TPU v7x, 768 devices: a whole 4x8x12 slice. The times are simulated.
768 devices in a mesh: row: 12 (over z_lo, core), col: 64 (over x, y, z_hi).
Axes of the slice: x: 4, y: 8, z: 12 (z_hi: 2, z_lo: 6; z = z_hi * 6 + z_lo), core: 2. Of those that a mesh axis runs over, the one named last changes fastest.
Arguments:
- x_window: float32 [1536, 122880], P('row', 'col'), may hold values from -6 to 6
- square_rows: float32 [3072, 122880], P('row', 'col'), may hold values from -0.3125 to 0.3125
- block_rank: int32 [12, 960], P('row', 'col'), may hold values from 0 to 14, as said below
- block_count: int32 [12, 64], P('row', 'col'), may hold values from 3 to 15, as said below
- panel_order: int32 [3], replicated, may hold values from 0 to 23, as said below
Outputs:
- updated: float32 [1536, 122880], P('row', 'col')
- total_square: float32 [], replicated
Inputs may be any that keep to these rules, and one draw needn't show every extreme that they name: `block_rank`: in each tile the 15 ranks are a permutation of 0 to 14; blocks in block columns of the form k(w) take the lowest ranks of their tile. `block_count`: skewed over tiles; some tile is full. `panel_order`: distinct values; the largest window row is always among them.
All inputs are finite; a program needn't handle non-finite values.
Results may differ from a plain program's by a relative error of at most 0.00045.
Values sent between devices are 32-bit elements; how exact they have to be, the bound alone decides.
A program may use at most 32 MiB of HBM per device.

v0:
```python
import jax
import jax.numpy as jnp
from jax import lax
from jax.sharding import PartitionSpec as P

BLOCK_WIDTH = 128
TILE_COLS = 15
WIN_ROWS = 2
ROUNDS = 3


def spread(value, axis, source):
    kept = jnp.where(lax.axis_index(axis) == source, value, 0).astype(value.dtype)
    return lax.psum(kept, axis)


def apply_live(values, live):
    slab = values.shape[0] // BLOCK_WIDTH
    shaped = values.reshape(slab, BLOCK_WIDTH, TILE_COLS, BLOCK_WIDTH)
    return (shaped * live[:, None, :, None]).reshape(values.shape)


def on_device(x_window, square_rows, block_rank, block_count, panel_order):
    col_count = lax.axis_size("col")
    row_count = lax.axis_size("row")
    all_blocks = TILE_COLS * col_count
    live = (block_rank < block_count[0, 0]).astype(jnp.float32)
    filtered = apply_live(x_window, live)
    product = jnp.zeros(x_window.shape, jnp.float32)
    for step in range(ROUNDS):
        fetch_window = panel_order[step]
        column = fetch_window * all_blocks // (WIN_ROWS * row_count)
        owner = column // TILE_COLS
        fetch_local = column % TILE_COLS
        piece = lax.dynamic_slice_in_dim(filtered, fetch_local * BLOCK_WIDTH, BLOCK_WIDTH, 1)
        left = spread(piece, "col", owner)
        window = panel_order[step]
        local = window % WIN_ROWS
        owner = window // WIN_ROWS
        piece = lax.dynamic_slice_in_dim(square_rows, local * BLOCK_WIDTH, BLOCK_WIDTH, 0)
        right = spread(piece, "row", owner)
        product = product + jnp.dot(
            left, right, preferred_element_type=jnp.float32, precision=lax.Precision.HIGHEST
        )
    update = apply_live(1.5 * filtered - 0.5 * product, live)
    total = lax.psum(jnp.sum(update * update), ("row", "col"))
    return (update, total)


def solution(mesh):
    return jax.shard_map(
        on_device,
        mesh=mesh,
        in_specs=(P("row", "col"), P("row", "col"), P("row", "col"), P("row", "col"), P()),
        out_specs=(P("row", "col"), P()),
        check_vma=False,
    )
```

profile of v0, /device:TPU:1, one launch (start us, length us, event | category | flops | bytes accessed | tf_op | source)
XLA Modules:
  0.0 1231.5 jit_solution(1141153022365976630)
XLA Ops:
  7.2 0.0 copy-start
  7.2 0.0 all-reduce.5.cloned.1.call-start
  7.2 1.5 fusion.4
  11.5 0.7 fusion.3
  12.1 0.1 broadcast_bitcast_fusion
  12.2 1.3 broadcast_multiply_fusion
  13.5 0.7 dynamic-slice_select_fusion.3
  14.1 0.0 all-reduce.5.cloned.1.call-update
  14.2 0.0 all-reduce.7.cloned.1.call-start
  22.1 0.0 copy-done
  22.1 1.7 dynamic-slice_select_fusion
  23.8 0.0 all-reduce.7.cloned.1.call-update
  23.8 901.2 %all-reduce.5.cloned.1.call-done = (f32[128,128]{1,0:T(8,128)}, f32[128,128]{1,0:T(8,128)}, f32[128,128]{1,0:T(8,128)}) async-done(((f32[128,128]{1,0:T(8,128)}, f32[128,128]{1,0:T(8,128)}, f32[128,128]{1,0:T(8,128)}), (f32[128,128]{1,0:T(8,128)}, f32[128,128]{1,0:T(8,128)}, f32[128,128]{1,0:T(8,128)})) %all-reduce.5.cloned.1.call-update) | async-done | bytes 196624 | tf_op jit(solution)/shard_map/psum | solution.py:14
  925.1 182.3 %all-reduce.7.cloned.1.call-done = (f32[128,1920]{1,0:T(8,128)}, f32[128,1920]{1,0:T(8,128)}, f32[128,1920]{1,0:T(8,128)}) async-done(((f32[128,1920]{1,0:T(8,128)}, f32[128,1920]{1,0:T(8,128)}, f32[128,1920]{1,0:T(8,128)}), (f32[128,1920]{1,0:T(8,128)}, f32[128,1920]{1,0:T(8,128)}, f32[128,1920]{1,0:T(8,128)})) %all-reduce.7.cloned.1.call-update) | async-done | bytes 2949136 | tf_op jit(solution)/shard_map/psum | solution.py:14
  1107.4 2.2 fusion.5
  1109.6 0.0 copy-start.1
  1109.6 0.0 copy-start.3
  1109.6 0.0 copy-start.4
  1109.7 0.0 copy-done.5
  1109.7 0.9 convolution_add_fusion.1
  1110.6 0.2 copy-done.1
  1110.8 0.3 copy-done.3
  1111.1 2.6 multiply_reduce_fusion
  1113.8 110.9 %psum.55 = f32[]{:T(128)} all-reduce(f32[]{:T(128)} %get-tuple-element.17), channel_id=1, replica_groups=mesh['row'=12,'col'=64] {'row','col'}, use_global_device_ids=true, to_apply=%region_7.8 | all-reduce | flops 1 | bytes 8 | tf_op jit(solution)/shard_map/psum | solution.py:46
  (4 shorter events, 0.0 us)
Async XLA Ops:
  7.2 15.0 %copy-start = (f32[256,1920]{1,0:T(8,128)S(1)}, f32[256,1920]{1,0:T(8,128)}, u32[]{:S(2)}) copy-start(f32[256,1920]{1,0:T(8,128)} %param.6) | copy-start | bytes 5898244
  7.2 917.9 %all-reduce.5.cloned.1.call-start = ((), (), s32[]{:S(2)}) async-start(), calls=%async_computation | async-start | bytes 393216 | tf_op jit(solution)/shard_map/psum | solution.py:14
  14.2 1093.2 %all-reduce.7.cloned.1.call-start = ((), (), s32[]{:S(2)}) async-start(), calls=%async_computation.1 | async-start | bytes 5898240 | tf_op jit(solution)/shard_map/psum | solution.py:14
  925.1 184.6 %copy-start.5 = (f32[128,128]{1,0:T(8,128)S(1)}, f32[128,128]{1,0:T(8,128)}, u32[]{:S(2)}) copy-start(f32[128,128]{1,0:T(8,128)} %get-tuple-element.3) | copy-start | bytes 196612
  1107.4 2.3 copy-start.2
  1109.6 1.2 copy-start.1
  1109.6 1.5 copy-start.3
  1109.6 1.5 copy-start.4
Sparse Core Ops, SparseCore 0:
  14.3 910.7 all-reduce.4
  929.5 177.7 all-reduce.6
where the time goes:
time: 1230 us
  waiting for transfers between devices  1080 us (88%)
  blocking collectives  111 us (9%)
  between operations  24.8 us (2%)
    psum x2, waiting for transfers between devices, spread(): return lax.psum(kept, axis)  1080 us
    psum x1, blocking collectives, on_device(): total = lax.psum(jnp.sum(update * update), ('row', 'col'))  111 us
  transfers between devices with their start and end apart: 2, of which 2 were waited for; matrix products, arithmetic and copies ran while one was open for 0% of the time, Pallas kernels for 0%

commit v1 on v0

v1 whole, which is shorter than its diff:
```python
import functools

import jax
import jax.numpy as jnp
from jax import lax
from jax.experimental import pallas as pl
from jax.experimental.pallas import tpu as pltpu
from jax.sharding import PartitionSpec as P

BLOCK = 128
HALF = 64
TILE_COLS = 15
ROUNDS = 3
UNITS = TILE_COLS * ROUNDS
CHIPS = 6
N_X, N_Y, N_Z = 4, 8, 12
LAST = 23
PIECE = BLOCK // N_Y
LAG = 4
SIB_LAG = 2
PHASES = (9, 15, 24, 30, 38)
MM_FIRST = PHASES[-1]
STEPS = UNITS + (CHIPS - 1) * LAG + SIB_LAG
MESH = pl.DeviceIdType.MESH


def kernel(
    panel, rank, count, x_hbm, sq_hbm, out_hbm, total,
    xv, win, up, down, panels, out, lsrc, pa, pb, pc, pd, pe, ph, left,
    acc, qs, qz, qy, qx,
    load_sem, win_sem, wsend, wrecv,
    up_s, up_r, dn_s, dn_r, sib_s, sib_r,
    p1_s, p1_r, p2_s, p2_r, p3_s, p3_r, p4_s, p4_r, p5_s, p5_r,
    qs_s, qs_r, qz_s, qz_r, qy_s, qy_r, qx_s, qx_r,
):
    row = lax.axis_index("row")
    col = lax.axis_index("col")
    chip, core = row // 2, row % 2
    zh = col % 2
    y = (col // 2) % N_Y
    x = col // (2 * N_Y)
    z = zh * CHIPS + chip

    def at_z(zz):
        return ((zz % CHIPS) * 2 + core, (x * N_Y + y) * 2 + zz // CHIPS)

    def at_y(yy):
        return (row, (x * N_Y + yy) * 2 + zh)

    def at_x(xx):
        return (row, (xx * N_Y + y) * 2 + zh)

    sibling = (chip * 2 + 1 - core, col)
    z_peers = [at_z(lax.rem(z + d, N_Z)) for d in range(1, N_Z)]
    y_peers = [at_y(lax.rem(y + d, N_Y)) for d in range(1, N_Y)]
    x_peers = [at_x(lax.rem(x + d, N_X)) for d in range(1, N_X)]
    other_zh = (row, (x * N_Y + y) * 2 + 1 - zh)
    above = (row + 2, col)
    below = (row - 2, col)

    def remote(src, dst, send, recv, device):
        return pltpu.make_async_remote_copy(
            src_ref=src, dst_ref=dst, send_sem=send, recv_sem=recv,
            device_id=device, device_id_type=MESH,
        )

    barrier = pltpu.get_barrier_semaphore()
    everyone = [sibling] + z_peers + y_peers + x_peers
    for peer in everyone:
        pl.semaphore_signal(barrier, inc=1, device_id=peer, device_id_type=MESH)

    x_load = pltpu.make_async_copy(x_hbm, xv, load_sem.at[0])
    x_load.start()
    cuts = ((0, 3 * BLOCK), (3 * BLOCK, 12 * BLOCK))
    win_loads, win_sends = [], []
    for part, (first, width) in enumerate(cuts):
        for w in range(2):
            win_loads.append(pltpu.make_async_copy(
                sq_hbm.at[pl.ds(w * BLOCK + core * HALF, HALF), pl.ds(first, width)],
                win.at[2 * core + w, :, pl.ds(first, width)],
                win_sem.at[part, w],
            ))
            win_sends.append(remote(
                sq_hbm.at[pl.ds(w * BLOCK + (1 - core) * HALF, HALF), pl.ds(first, width)],
                win.at[2 * core + w, :, pl.ds(first, width)],
                wsend.at[part, w], wrecv.at[part, w], sibling,
            ))

    def win_arrival(part, w):
        first, width = cuts[part]
        dst = win.at[2 * (1 - core) + w, :, pl.ds(first, width)]
        return remote(dst, dst, wsend.at[part, w], wrecv.at[part, w], sibling)

    for copy in win_loads:
        copy.start()

    p0, p1, p2 = panel[0], panel[1], panel[2]
    q0 = jnp.where(p0 == LAST, p1, p0)
    q1 = jnp.where(p2 == LAST, p1, p2)
    q = (q0, q1, jnp.int32(LAST))
    owner_col = [(8 * w) // 3 for w in q]

    cand = (3 * col + 7) // 8
    place = jnp.minimum(40 * cand - TILE_COLS * col, TILE_COLS - 1)
    x_load.wait()
    cand_live = rank[0, place] < count[0, 0]
    lsrc[...] = jnp.where(
        cand_live, xv[:, pl.ds(pl.multiple_of(place * BLOCK, BLOCK), BLOCK)], 0.0
    )

    pl.semaphore_wait(barrier, len(everyone))

    for copy in win_sends:
        copy.start()

    def p1_copy(d):
        to = lax.rem(y + d, N_Y)
        return remote(
            lsrc.at[pl.ds(to * PIECE, PIECE)], pa.at[y], p1_s.at[d - 1], p1_r.at[d - 1], at_y(to)
        )

    def p1_wait(d):
        frm = lax.rem(y + N_Y - d, N_Y)
        return remote(pa.at[frm], pa.at[frm], p1_s.at[d - 1], p1_r.at[d - 1], at_y(frm))

    for d in range(1, N_Y):
        p1_copy(d).start()
    pa[y] = lsrc[pl.ds(pl.multiple_of(y * PIECE, PIECE), PIECE), :]

    def p2_copy(t):
        return remote(pb.at[t], pc.at[x], p2_s.at[t], p2_r.at[x], at_x(t))

    def p2_wait(frm):
        return remote(pc.at[frm], pc.at[frm], p2_s.at[0], p2_r.at[frm], at_x(frm))

    def p3_copy():
        return remote(pd, pe, p3_s.at[0], p3_r.at[0], other_zh)

    def p4_slot(t):
        return ph.at[:, pl.ds(pl.multiple_of(t * BLOCK, BLOCK), BLOCK)]

    def p4_copy(d):
        return remote(
            p4_slot(x), p4_slot(x), p4_s.at[d - 1], p4_r.at[d - 1], at_x(lax.rem(x + d, N_X))
        )

    def p4_wait(d):
        frm = lax.rem(x + N_X - d, N_X)
        return remote(p4_slot(frm), p4_slot(frm), p4_s.at[d - 1], p4_r.at[d - 1], at_x(frm))

    def left_rows(yy):
        return left.at[pl.ds(pl.multiple_of(yy * PIECE, PIECE), PIECE), :]

    def p5_copy(d):
        return remote(
            ph, left_rows(y), p5_s.at[d - 1], p5_r.at[d - 1], at_y(lax.rem(y + d, N_Y))
        )

    def p5_wait(d):
        frm = lax.rem(y + N_Y - d, N_Y)
        return remote(left_rows(frm), left_rows(frm), p5_s.at[d - 1], p5_r.at[d - 1], at_y(frm))

    def phase_1_to_2():
        for d in range(1, N_Y):
            p1_wait(d).wait_recv()
        for t in range(ROUNDS):
            pb[t] = pa[(owner_col[t] // 2) % N_Y]
        for t in range(ROUNDS):
            @pl.when(x != t)
            def _(t=t):
                p2_copy(t).start()

            @pl.when(x == t)
            def _(t=t):
                pc[t] = pb[t]

    my_owner = jnp.where(x == 0, owner_col[0], jnp.where(x == 1, owner_col[1], owner_col[2]))

    def phase_2_to_3():
        @pl.when(x < ROUNDS)
        def _():
            for frm in range(N_X):
                @pl.when(x != frm)
                def _(frm=frm):
                    p2_wait(frm).wait_recv()
            pd[...] = pc[my_owner // (2 * N_Y)]
            p3_copy().start()

    def phase_3_to_4():
        @pl.when(x < ROUNDS)
        def _():
            p3_copy().wait_recv()
            mine = jnp.where(my_owner % 2 == zh, pd[...], pe[...])
            ph[:, pl.ds(pl.multiple_of(x * BLOCK, BLOCK), BLOCK)] = mine
            for d in range(1, N_X):
                p4_copy(d).start()

    def phase_4_to_5():
        for d in range(1, N_X):
            @pl.when(lax.rem(x + N_X - d, N_X) < ROUNDS)
            def _(d=d):
                p4_wait(d).wait_recv()
        left[pl.ds(pl.multiple_of(y * PIECE, PIECE), PIECE), :] = ph[...]
        for d in range(1, N_Y):
            p5_copy(d).start()

    def phase_5_end():
        for d in range(1, N_Y):
            p5_wait(d).wait_recv()

    def up_copy(u):
        return remote(up.at[u], up.at[u], up_s.at[u], up_r.at[u], above)

    def down_copy(u):
        return remote(down.at[u], down.at[u], dn_s.at[u], dn_r.at[u], below)

    def sib_slot(u, half):
        return panels.at[u, pl.ds(pl.multiple_of(half * HALF, HALF), HALF), :]

    def sib_copy(u):
        return remote(sib_slot(u, core), sib_slot(u, core), sib_s.at[u], sib_r.at[u], sibling)

    def sib_wait(u):
        return remote(
            sib_slot(u, 1 - core), sib_slot(u, 1 - core), sib_s.at[u], sib_r.at[u], sibling
        )

    def window_of(t):
        return jnp.where(t == 0, q[0], jnp.where(t == 1, q[1], q[2]))

    def inject(buf, u):
        j, t = u // ROUNDS, u % ROUNDS
        w = window_of(t)
        cols = pl.ds(pl.multiple_of(j * BLOCK, BLOCK), BLOCK)
        value = buf[u]
        for k in range(4):
            value = jnp.where(w == 4 * chip + k, win[k, :, cols], value)
        buf[u] = value

    far = jnp.maximum(chip, CHIPS - 1 - chip)
    acc[...] = jnp.zeros_like(acc)

    for w in range(2):
        win_loads[w].wait()
        win_arrival(0, w).wait_recv()

    def multiply(j):
        for t in range(ROUNDS):
            sib_wait(j * ROUNDS + t).wait_recv()
        right = panels[pl.ds(j * ROUNDS, ROUNDS)].reshape(ROUNDS * BLOCK, BLOCK)
        product = jnp.dot(
            left[...], right, preferred_element_type=jnp.float32, precision=lax.Precision.HIGHEST
        )
        cols = pl.ds(pl.multiple_of(j * BLOCK, BLOCK), BLOCK)
        live = rank[0, j] < count[0, 0]
        update = jnp.where(live, 1.5 * xv[:, cols] - 0.5 * product, 0.0)
        out[:, cols] = update
        acc[...] += jnp.sum((update * update).reshape(BLOCK // 8, 8, BLOCK), axis=0)

    def step(s, j):
        @pl.when(s == 9)
        def _():
            for w in range(2):
                win_loads[2 + w].wait()
                win_arrival(1, w).wait_recv()

        u = s - chip * LAG

        @pl.when((u >= 0) & (u < UNITS) & (lax.rem(u + ROUNDS * 40, ROUNDS) < 2))
        def _():
            @pl.when(chip > 0)
            def _():
                up_copy(u).wait_recv()

            inject(up, u)

            @pl.when(chip < CHIPS - 1)
            def _():
                up_copy(u).start()

        d = s - (CHIPS - 1 - chip) * LAG

        @pl.when((d >= 0) & (d < UNITS))
        def _():
            @pl.when(chip < CHIPS - 1)
            def _():
                down_copy(d).wait_recv()

            inject(down, d)

            @pl.when(chip > 0)
            def _():
                down_copy(d).start()

        f = s - far * LAG

        @pl.when((f >= 0) & (f < UNITS))
        def _():
            t = f % ROUNDS
            from_up = window_of(t) // 4 < chip
            panels[f, pl.ds(pl.multiple_of(core * HALF, HALF), HALF), :] = jnp.where(
                from_up, up[f], down[f]
            )
            sib_copy(f).start()

        for at, phase in zip(
            PHASES, (phase_1_to_2, phase_2_to_3, phase_3_to_4, phase_4_to_5, phase_5_end)
        ):
            pl.when(s == at)(phase)

        ready = (
            (j < TILE_COLS)
            & (s >= MM_FIRST + 2 * j)
            & (s >= ROUNDS * j + ROUNDS - 1 + far * LAG + SIB_LAG)
        )

        @pl.when(ready)
        def _():
            multiply(j)

        return j + ready.astype(jnp.int32)

    lax.fori_loop(0, STEPS, step, jnp.int32(0))

    store = pltpu.make_async_copy(out, out_hbm, load_sem.at[1])
    store.start()

    sib_sum = remote(acc, qs.at[0], qs_s.at[0], qs_r.at[0], sibling)
    sib_sum.start()

    for copy in win_sends:
        copy.wait_send()
    for d in range(1, N_Y):
        p1_copy(d).wait_send()
        p5_copy(d).wait_send()
    for t in range(ROUNDS):
        @pl.when(x != t)
        def _(t=t):
            p2_copy(t).wait_send()

    @pl.when(x < ROUNDS)
    def _():
        p3_copy().wait_send()
        for d in range(1, N_X):
            p4_copy(d).wait_send()

    sib_sum.wait()
    qz[z] = acc[...] + qs[0]
    z_sums = [
        remote(qz.at[z], qz.at[z], qz_s.at[d - 1], qz_r.at[d - 1], peer)
        for d, peer in enumerate(z_peers, 1)
    ]
    for copy in z_sums:
        copy.start()

    def drain(u, carry):
        sib_copy(u).wait_send()

        @pl.when((chip < CHIPS - 1) & (u % ROUNDS < 2))
        def _():
            up_copy(u).wait_send()

        @pl.when(chip > 0)
        def _():
            down_copy(u).wait_send()

        return carry

    lax.fori_loop(0, UNITS, drain, 0)

    for d in range(1, N_Z):
        frm = lax.rem(z + N_Z - d, N_Z)
        remote(qz.at[frm], qz.at[frm], qz_s.at[d - 1], qz_r.at[d - 1], at_z(frm)).wait_recv()
    qy[y] = jnp.sum(qz[...], axis=0)
    y_sums = [
        remote(qy.at[y], qy.at[y], qy_s.at[d - 1], qy_r.at[d - 1], peer)
        for d, peer in enumerate(y_peers, 1)
    ]
    for copy in y_sums:
        copy.start()
    for d in range(1, N_Y):
        frm = lax.rem(y + N_Y - d, N_Y)
        remote(qy.at[frm], qy.at[frm], qy_s.at[d - 1], qy_r.at[d - 1], at_y(frm)).wait_recv()
    qx[x] = jnp.sum(qy[...], axis=0)
    x_sums = [
        remote(qx.at[x], qx.at[x], qx_s.at[d - 1], qx_r.at[d - 1], peer)
        for d, peer in enumerate(x_peers, 1)
    ]
    for copy in x_sums:
        copy.start()
    for d in range(1, N_X):
        frm = lax.rem(x + N_X - d, N_X)
        remote(qx.at[frm], qx.at[frm], qx_s.at[d - 1], qx_r.at[d - 1], at_x(frm)).wait_recv()
    total[0, 0] = jnp.sum(jnp.sum(qx[...], axis=0))
    for copy in z_sums + y_sums + x_sums:
        copy.wait_send()
    store.wait()


def on_device(x_window, square_rows, block_rank, block_count, panel_order):
    width = TILE_COLS * BLOCK
    vmem = lambda *shape: pltpu.VMEM(shape, jnp.float32)
    dma = lambda *shape: pltpu.SemaphoreType.DMA(shape)
    updated, total = pl.pallas_call(
        kernel,
        out_shape=(
            jax.ShapeDtypeStruct((BLOCK, width), jnp.float32),
            jax.ShapeDtypeStruct((1, 1), jnp.float32),
        ),
        in_specs=[pl.BlockSpec(memory_space=pltpu.SMEM)] * 3
        + [pl.BlockSpec(memory_space=pl.ANY)] * 2,
        out_specs=(
            pl.BlockSpec(memory_space=pl.ANY),
            pl.BlockSpec(memory_space=pltpu.SMEM),
        ),
        scratch_shapes=[
            vmem(BLOCK, width),
            vmem(4, HALF, width),
            vmem(UNITS, HALF, BLOCK),
            vmem(UNITS, HALF, BLOCK),
            vmem(UNITS, BLOCK, BLOCK),
            vmem(BLOCK, width),
            vmem(BLOCK, BLOCK),
            vmem(N_Y, PIECE, BLOCK),
            vmem(ROUNDS, PIECE, BLOCK),
            vmem(N_X, PIECE, BLOCK),
            vmem(PIECE, BLOCK),
            vmem(PIECE, BLOCK),
            vmem(PIECE, ROUNDS * BLOCK),
            vmem(BLOCK, ROUNDS * BLOCK),
            vmem(8, BLOCK),
            vmem(1, 8, BLOCK),
            vmem(N_Z, 8, BLOCK),
            vmem(N_Y, 8, BLOCK),
            vmem(N_X, 8, BLOCK),
            dma(2), dma(2, 2), dma(2, 2), dma(2, 2),
            dma(UNITS), dma(UNITS), dma(UNITS), dma(UNITS), dma(UNITS), dma(UNITS),
            dma(N_Y - 1), dma(N_Y - 1), dma(ROUNDS), dma(N_X), dma(1), dma(1),
            dma(N_X - 1), dma(N_X - 1), dma(N_Y - 1), dma(N_Y - 1),
            dma(1), dma(1), dma(N_Z - 1), dma(N_Z - 1),
            dma(N_Y - 1), dma(N_Y - 1), dma(N_X - 1), dma(N_X - 1),
        ],
        compiler_params=pltpu.CompilerParams(
            collective_id=0, has_side_effects=True, vmem_limit_bytes=40 << 20
        ),
        name="sign_window",
    )(panel_order, block_rank, block_count, x_window, square_rows)
    return updated, total[0, 0]


def solution(mesh):
    return jax.shard_map(
        on_device,
        mesh=mesh,
        in_specs=(P("row", "col"), P("row", "col"), P("row", "col"), P("row", "col"), P()),
        out_specs=(P("row", "col"), P()),
        check_vma=False,
    )
```

time: 1230 us -> 101 us (0.08)
  waiting for transfers between devices: 1080 us -> 0 us
  blocking collectives: 111 us -> 0 us
  Pallas kernels: 0 us -> 92.3 us
  between operations: 24.8 us -> 3.04 us
    psum x2 -> x0, waiting for transfers between devices: 1080 us -> none  [spread(): return lax.psum(kept, axis)]
    psum x1 -> x0, blocking collectives: 111 us -> none  [on_device(): total = lax.psum(jnp.sum(update * update), ('row', 'col'))]
    pallas_call x0 -> x1, Pallas kernels: none -> 92.3 us  [on_device(): pl.pallas_call(kernel, out_shape=(jax.ShapeDtypeStruct((BLOCK, width), jn...]
  transfers between devices with their start and end apart: 2 -> 0, of which waited for: 2 -> 0; matrix products, arithmetic and copies ran while one was open for 0% -> 0% of each run, Pallas kernels for 0% -> 0%
where the time goes in v1:
time: 101 us; the launch traced here: 100 us
  Pallas kernels  92.3 us (91%)
  local copies, waits for them, and re-layouts  5 us (5%)
  between operations  3.04 us (3%)
    pallas_call x1, Pallas kernels, on_device(): pl.pallas_call(kernel, out_shape=(jax.ShapeDtypeStruct((BLOCK, width), jn...  92.3 us
    unnamed x9, local copies, waits for them, and re-layouts  5 us

profile of v1, /device:TPU:1, one launch (start us, length us, event | category | flops | bytes accessed | tf_op | source)
XLA Modules:
  0.0 100.3 jit_solution(1190031332092743961)
XLA Ops:
  1.3 0.0 copy-start
  1.3 1.5 %copy-done = f32[256,1920]{1,0:T(8,128)S(1)} copy-done((f32[256,1920]{1,0:T(8,128)S(1)}, f32[256,1920]{1,0:T(8,128)}, u32[]{:S(2)}) %copy-start) | copy-done | bytes 1966104
  2.8 0.0 copy-start.1
  2.8 1.2 %copy-done.1 = f32[128,1920]{1,0:T(8,128)S(1)} copy-done((f32[128,1920]{1,0:T(8,128)S(1)}, f32[128,1920]{1,0:T(8,128)}, u32[]{:S(2)}) %copy-start.1) | copy-done | bytes 983064
  4.0 0.0 copy-start.2
  4.0 0.7 copy-done.2
  4.7 0.0 copy-start.3
  4.7 0.7 copy-done.3
  5.3 92.3 %sign_window.1 = (f32[128,1920]{1,0:T(8,128)S(1)}, f32[1,1]{1,0:T(1,128)}) custom-call(s32[3]{0:T(128)S(1)} %copy-done.2, s32[1,15]{1,0:T(1,128)S(1)} %copy-done.3, s32[1,1]{1,0:T(1,128)S(6)} %copy.9.count, f32[128,1920]{1,0:T(8,128)S(1)} %copy-done.1, f32[256,1920]{1,0:T(8,128)S(1)} %copy-done), custom_call_target="tpu_custom_call" | custom-call | tf_op jit(solution)/shard_map/sign_window/pallas_call | solution.py:404
  97.6 0.9 copy.10
Async XLA Ops:
  1.3 1.5 %copy-start = (f32[256,1920]{1,0:T(8,128)S(1)}, f32[256,1920]{1,0:T(8,128)}, u32[]{:S(2)}) copy-start(f32[256,1920]{1,0:T(8,128)} %sq_hbm.1) | copy-start | bytes 5898244
  2.8 1.2 %copy-start.1 = (f32[128,1920]{1,0:T(8,128)S(1)}, f32[128,1920]{1,0:T(8,128)}, u32[]{:S(2)}) copy-start(f32[128,1920]{1,0:T(8,128)} %x_hbm.1) | copy-start | bytes 2949124
  4.0 0.7 copy-start.2
  4.7 0.7 copy-start.3

commit v2 on v1

--- a/solution.py
+++ b/solution.py
@@ -16,20 +16,29 @@
 N_X, N_Y, N_Z = 4, 8, 12
 LAST = 23
 PIECE = BLOCK // N_Y
-LAG = 4
+FAR_Z = (6, 5, 7, 4, 8, 3, 9, 2, 10, 1, 11)
+FAR_Y = (4, 3, 5, 2, 6, 1, 7)
+FAR_X = (2, 1, 3)
+LAG = 6
 SIB_LAG = 2
-PHASES = (9, 15, 24, 30, 38)
+PHASES = (12, 20, 30, 37, 44)
 MM_FIRST = PHASES[-1]
-STEPS = UNITS + (CHIPS - 1) * LAG + SIB_LAG
+WRAPS = 5
+WRAP_FIRST = 7
+DOWN_LAST = TILE_COLS - WRAPS
+TRIPLES = WRAP_FIRST + WRAPS
+SLOTS = 3 * TRIPLES + 2 * (TILE_COLS - TRIPLES)
+RELAY_STEP = 18
+STEPS = SLOTS + (CHIPS - 1) * LAG + SIB_LAG
 MESH = pl.DeviceIdType.MESH
 
 
 def kernel(
     panel, rank, count, x_hbm, sq_hbm, out_hbm, total,
-    xv, win, up, down, panels, out, lsrc, pa, pb, pc, pd, pe, ph, left,
+    xv, win, up, down, relay, panels, out, lsrc, pa, pb, pc, pd, pe, ph, left,
     acc, qs, qz, qy, qx,
     load_sem, win_sem, wsend, wrecv,
-    up_s, up_r, dn_s, dn_r, sib_s, sib_r,
+    up_s, up_r, dn_s, dn_r, rl_s, rl_r, wr_s, sib_s, sib_r,
     p1_s, p1_r, p2_s, p2_r, p3_s, p3_r, p4_s, p4_r, p5_s, p5_r,
     qs_s, qs_r, qz_s, qz_r, qy_s, qy_r, qx_s, qx_r,
 ):
@@ -51,9 +60,9 @@
         return (row, (xx * N_Y + y) * 2 + zh)
 
     sibling = (chip * 2 + 1 - core, col)
-    z_peers = [at_z(lax.rem(z + d, N_Z)) for d in range(1, N_Z)]
-    y_peers = [at_y(lax.rem(y + d, N_Y)) for d in range(1, N_Y)]
-    x_peers = [at_x(lax.rem(x + d, N_X)) for d in range(1, N_X)]
+    z_peers = [at_z(lax.rem(z + d, N_Z)) for d in FAR_Z]
+    y_peers = [at_y(lax.rem(y + d, N_Y)) for d in FAR_Y]
+    x_peers = [at_x(lax.rem(x + d, N_X)) for d in FAR_X]
     other_zh = (row, (x * N_Y + y) * 2 + 1 - zh)
     above = (row + 2, col)
     below = (row - 2, col)
@@ -123,7 +132,7 @@
         frm = lax.rem(y + N_Y - d, N_Y)
         return remote(pa.at[frm], pa.at[frm], p1_s.at[d - 1], p1_r.at[d - 1], at_y(frm))
 
-    for d in range(1, N_Y):
+    for d in FAR_Y:
         p1_copy(d).start()
     pa[y] = lsrc[pl.ds(pl.multiple_of(y * PIECE, PIECE), PIECE), :]
 
@@ -201,7 +210,7 @@
             def _(d=d):
                 p4_wait(d).wait_recv()
         left[pl.ds(pl.multiple_of(y * PIECE, PIECE), PIECE), :] = ph[...]
-        for d in range(1, N_Y):
+        for d in FAR_Y:
             p5_copy(d).start()
 
     def phase_5_end():
@@ -228,14 +237,34 @@
     def window_of(t):
         return jnp.where(t == 0, q[0], jnp.where(t == 1, q[1], q[2]))
 
+    def slot_of(u):
+        late = u - 3 * TRIPLES
+        j = jnp.where(late < 0, u // 3, TRIPLES + jnp.maximum(late, 0) // 2)
+        t = jnp.where(late < 0, u % 3, jnp.maximum(late, 0) % 2)
+        return j, t
+
+    def columns(j):
+        return pl.ds(pl.multiple_of(j * BLOCK, BLOCK), BLOCK)
+
     def inject(buf, u):
-        j, t = u // ROUNDS, u % ROUNDS
+        j, t = slot_of(u)
         w = window_of(t)
-        cols = pl.ds(pl.multiple_of(j * BLOCK, BLOCK), BLOCK)
         value = buf[u]
         for k in range(4):
-            value = jnp.where(w == 4 * chip + k, win[k, :, cols], value)
+            value = jnp.where(w == 4 * chip + k, win[k, :, columns(j)], value)
         buf[u] = value
+
+    def wrap_copy(n):
+        return remote(
+            win.at[3, :, pl.ds((DOWN_LAST + n) * BLOCK, BLOCK)], relay.at[n],
+            wr_s.at[n], rl_r.at[n], at_z(lax.rem(z + 4, N_Z)),
+        )
+
+    def relay_copy(n):
+        slot = 3 * (WRAP_FIRST + n) + 2
+        return remote(
+            relay.at[n], up.at[slot], rl_s.at[n], up_r.at[slot], at_z(lax.rem(z + 3, N_Z))
+        )
 
     far = jnp.maximum(chip, CHIPS - 1 - chip)
     acc[...] = jnp.zeros_like(acc)
@@ -264,9 +293,23 @@
                 win_loads[2 + w].wait()
                 win_arrival(1, w).wait_recv()
 
+        @pl.when((s == 10) & (chip == CHIPS - 1))
+        def _():
+            for n in range(WRAPS):
+                wrap_copy(n).start()
+
+        for n in range(WRAPS):
+            @pl.when((s == RELAY_STEP + 2 * n) & (chip == 3))
+            def _(n=n):
+                remote(
+                    relay.at[n], relay.at[n], wr_s.at[n], rl_r.at[n], at_z(lax.rem(z + 8, N_Z))
+                ).wait_recv()
+                relay_copy(n).start()
+
         u = s - chip * LAG
-
-        @pl.when((u >= 0) & (u < UNITS) & (lax.rem(u + ROUNDS * 40, ROUNDS) < 2))
+        uj, ut = slot_of(jnp.clip(u, 0, SLOTS - 1))
+
+        @pl.when((u >= 0) & (u < SLOTS) & (ut < 2))
         def _():
             @pl.when(chip > 0)
             def _():
@@ -278,9 +321,18 @@
             def _():
                 up_copy(u).start()
 
+        @pl.when((u >= 0) & (u < SLOTS) & (ut == 2) & (uj >= WRAP_FIRST) & (chip < CHIPS - 1))
+        def _():
+            up_copy(u).wait_recv()
+
+            @pl.when(chip < CHIPS - 2)
+            def _():
+                up_copy(u).start()
+
         d = s - (CHIPS - 1 - chip) * LAG
-
-        @pl.when((d >= 0) & (d < UNITS))
+        dj, dt = slot_of(jnp.clip(d, 0, SLOTS - 1))
+
+        @pl.when((d >= 0) & (d < SLOTS) & ((dt < 2) | (dj < DOWN_LAST)))
         def _():
             @pl.when(chip < CHIPS - 1)
             def _():
@@ -294,14 +346,27 @@
 
         f = s - far * LAG
 
-        @pl.when((f >= 0) & (f < UNITS))
-        def _():
-            t = f % ROUNDS
-            from_up = window_of(t) // 4 < chip
-            panels[f, pl.ds(pl.multiple_of(core * HALF, HALF), HALF), :] = jnp.where(
-                from_up, up[f], down[f]
-            )
-            sib_copy(f).start()
+        fj, ft = slot_of(jnp.clip(f, 0, SLOTS - 1))
+
+        def finish(j, t, value):
+            unit = ROUNDS * j + t
+            panels[unit, pl.ds(pl.multiple_of(core * HALF, HALF), HALF), :] = value
+            sib_copy(unit).start()
+
+        @pl.when((f >= 0) & (f < SLOTS) & ((ft < 2) | (fj < DOWN_LAST)))
+        def _():
+            finish(fj, ft, jnp.where(window_of(ft) // 4 < chip, up[f], down[f]))
+
+        wraps = (f >= 0) & (f < SLOTS) & (ft == 2) & (fj >= WRAP_FIRST)
+        wrapped = fj + DOWN_LAST - WRAP_FIRST
+
+        @pl.when(wraps & (chip < CHIPS - 1))
+        def _():
+            finish(wrapped, 2, up[f])
+
+        @pl.when(wraps & (chip == CHIPS - 1))
+        def _():
+            finish(wrapped, 2, win[3, :, columns(wrapped)])
 
         for at, phase in zip(
             PHASES, (phase_1_to_2, phase_2_to_3, phase_3_to_4, phase_4_to_5, phase_5_end)
@@ -311,7 +376,7 @@
         ready = (
             (j < TILE_COLS)
             & (s >= MM_FIRST + 2 * j)
-            & (s >= ROUNDS * j + ROUNDS - 1 + far * LAG + SIB_LAG)
+            & (s >= jnp.minimum(3 * j + 2, 2 * j + TRIPLES + 1) + far * LAG + SIB_LAG)
         )
 
         @pl.when(ready)
@@ -348,25 +413,41 @@
     qz[z] = acc[...] + qs[0]
     z_sums = [
         remote(qz.at[z], qz.at[z], qz_s.at[d - 1], qz_r.at[d - 1], peer)
-        for d, peer in enumerate(z_peers, 1)
+        for d, peer in zip(FAR_Z, z_peers)
     ]
     for copy in z_sums:
         copy.start()
 
     def drain(u, carry):
+        j, t = slot_of(u)
+
+        @pl.when(
+            (chip < CHIPS - 1) & (t < 2) | (chip < CHIPS - 2) & (t == 2) & (j >= WRAP_FIRST)
+        )
+        def _():
+            up_copy(u).wait_send()
+
+        @pl.when((chip > 0) & ((t < 2) | (j < DOWN_LAST)))
+        def _():
+            down_copy(u).wait_send()
+
+        return carry
+
+    lax.fori_loop(0, SLOTS, drain, 0)
+
+    def drain_sib(u, carry):
         sib_copy(u).wait_send()
-
-        @pl.when((chip < CHIPS - 1) & (u % ROUNDS < 2))
-        def _():
-            up_copy(u).wait_send()
-
-        @pl.when(chip > 0)
-        def _():
-            down_copy(u).wait_send()
-
         return carry
 
-    lax.fori_loop(0, UNITS, drain, 0)
+    lax.fori_loop(0, UNITS, drain_sib, 0)
+    for n in range(WRAPS):
+        @pl.when(chip == CHIPS - 1)
+        def _(n=n):
+            wrap_copy(n).wait_send()
+
+        @pl.when(chip == 3)
+        def _(n=n):
+            relay_copy(n).wait_send()
 
     for d in range(1, N_Z):
         frm = lax.rem(z + N_Z - d, N_Z)
@@ -374,7 +455,7 @@
     qy[y] = jnp.sum(qz[...], axis=0)
     y_sums = [
         remote(qy.at[y], qy.at[y], qy_s.at[d - 1], qy_r.at[d - 1], peer)
-        for d, peer in enumerate(y_peers, 1)
+        for d, peer in zip(FAR_Y, y_peers)
     ]
     for copy in y_sums:
         copy.start()
@@ -384,7 +465,7 @@
     qx[x] = jnp.sum(qy[...], axis=0)
     x_sums = [
         remote(qx.at[x], qx.at[x], qx_s.at[d - 1], qx_r.at[d - 1], peer)
-        for d, peer in enumerate(x_peers, 1)
+        for d, peer in zip(FAR_X, x_peers)
     ]
     for copy in x_sums:
         copy.start()
@@ -416,8 +497,9 @@
         scratch_shapes=[
             vmem(BLOCK, width),
             vmem(4, HALF, width),
-            vmem(UNITS, HALF, BLOCK),
-            vmem(UNITS, HALF, BLOCK),
+            vmem(SLOTS, HALF, BLOCK),
+            vmem(SLOTS, HALF, BLOCK),
+            vmem(WRAPS, HALF, BLOCK),
             vmem(UNITS, BLOCK, BLOCK),
             vmem(BLOCK, width),
             vmem(BLOCK, BLOCK),
@@ -434,14 +516,15 @@
             vmem(N_Y, 8, BLOCK),
             vmem(N_X, 8, BLOCK),
             dma(2), dma(2, 2), dma(2, 2), dma(2, 2),
-            dma(UNITS), dma(UNITS), dma(UNITS), dma(UNITS), dma(UNITS), dma(UNITS),
+            dma(SLOTS), dma(SLOTS), dma(SLOTS), dma(SLOTS),
+            dma(WRAPS), dma(WRAPS), dma(WRAPS), dma(UNITS), dma(UNITS),
             dma(N_Y - 1), dma(N_Y - 1), dma(ROUNDS), dma(N_X), dma(1), dma(1),
             dma(N_X - 1), dma(N_X - 1), dma(N_Y - 1), dma(N_Y - 1),
             dma(1), dma(1), dma(N_Z - 1), dma(N_Z - 1),
             dma(N_Y - 1), dma(N_Y - 1), dma(N_X - 1), dma(N_X - 1),
         ],
         compiler_params=pltpu.CompilerParams(
-            collective_id=0, has_side_effects=True, vmem_limit_bytes=40 << 20
+            collective_id=0, has_side_effects=True, vmem_limit_bytes=62 << 20
         ),
         name="sign_window",
     )(panel_order, block_rank, block_count, x_window, square_rows)

time: 101 us -> 93.9 us (0.930)
  Pallas kernels: 92.3 us -> 87.5 us
  local copies, waits for them, and re-layouts: 5 us -> 2.21 us
    pallas_call x1, Pallas kernels: 92.3 us -> 87.5 us  [on_device(): pl.pallas_call(kernel, out_shape=(jax.ShapeDtypeStruct((BLOCK, width), jn...]
    unnamed x9 -> x1, local copies, waits for them, and re-layouts: 5 us -> 2.21 us
where the time goes in v2:
time: 93.9 us; the launch traced here: 92.6 us
  Pallas kernels  87.5 us (93%)
  between operations  2.96 us (3%)
  local copies, waits for them, and re-layouts  2.21 us (2%)
    pallas_call x1, Pallas kernels, on_device(): pl.pallas_call(kernel, out_shape=(jax.ShapeDtypeStruct((BLOCK, width), jn...  87.5 us
    unnamed x1, local copies, waits for them, and re-layouts  2.21 us

profile of v2, /device:TPU:1, one launch (start us, length us, event | category | flops | bytes accessed | tf_op | source)
XLA Modules:
  0.0 92.6 jit_solution(12809042796176377882)
XLA Ops:
  1.3 87.5 %sign_window.1 = (f32[128,1920]{1,0:T(8,128)}, f32[1,1]{1,0:T(1,128)}) custom-call(s32[3]{0:T(128)} %panel.1, s32[1,15]{1,0:T(1,128)} %rank.1, s32[1,1]{1,0:T(1,128)S(6)} %copy.9.count, f32[128,1920]{1,0:T(8,128)} %x_hbm.1, f32[256,1920]{1,0:T(8,128)} %sq_hbm.1), custom_call_target="tpu_custom_call" | custom-call | tf_op jit(solution)/shard_map/sign_window/pallas_call | solution.py:485
  88.7 2.2 %copy.10 = f32[128,1920]{1,0:T(8,128)} copy(f32[128,1920]{1,0:T(8,128)} %get-tuple-element.8) | data formatting | bytes 1966080

commit v3 on v2

--- a/solution.py
+++ b/solution.py
@@ -11,6 +11,8 @@
 HALF = 64
 TILE_COLS = 15
 ROUNDS = 3
+SUB = 1
+PART = HALF // SUB
 UNITS = TILE_COLS * ROUNDS
 CHIPS = 6
 N_X, N_Y, N_Z = 4, 8, 12
@@ -28,16 +30,17 @@
 DOWN_LAST = TILE_COLS - WRAPS
 TRIPLES = WRAP_FIRST + WRAPS
 SLOTS = 3 * TRIPLES + 2 * (TILE_COLS - TRIPLES)
-RELAY_STEP = 18
+RELAY_STEP = 22
 STEPS = SLOTS + (CHIPS - 1) * LAG + SIB_LAG
 MESH = pl.DeviceIdType.MESH
 
 
 def kernel(
-    panel, rank, count, x_hbm, sq_hbm, out_hbm, total,
-    xv, win, up, down, relay, panels, out, lsrc, pa, pb, pc, pd, pe, ph, left,
+    panel_hbm, rank_hbm, count_hbm, x_hbm, sq_hbm, out_hbm, total,
+    panel, rank, count,
+    xv, win, up, down, relay, panels, out, lsrc, pa, pb, pc, pd, pe, ph, left, left_high, left_low,
     acc, qs, qz, qy, qx,
-    load_sem, win_sem, wsend, wrecv,
+    small_sem, load_sem, win_sem, wsend, wrecv,
     up_s, up_r, dn_s, dn_r, rl_s, rl_r, wr_s, sib_s, sib_r,
     p1_s, p1_r, p2_s, p2_r, p3_s, p3_r, p4_s, p4_r, p5_s, p5_r,
     qs_s, qs_r, qz_s, qz_r, qy_s, qy_r, qx_s, qx_r,
@@ -73,13 +76,19 @@
             device_id=device, device_id_type=MESH,
         )
 
+    small_loads = [
+        pltpu.make_async_copy(src, dst, small_sem.at[n])
+        for n, (src, dst) in enumerate(((panel_hbm, panel), (rank_hbm, rank), (count_hbm, count)))
+    ]
+    for copy in small_loads:
+        copy.start()
+
     barrier = pltpu.get_barrier_semaphore()
-    everyone = [sibling] + z_peers + y_peers + x_peers
+    everyone = [sibling] + z_peers[::-1] + y_peers + x_peers
     for peer in everyone:
         pl.semaphore_signal(barrier, inc=1, device_id=peer, device_id_type=MESH)
 
     x_load = pltpu.make_async_copy(x_hbm, xv, load_sem.at[0])
-    x_load.start()
     cuts = ((0, 3 * BLOCK), (3 * BLOCK, 12 * BLOCK))
     win_loads, win_sends = [], []
     for part, (first, width) in enumerate(cuts):
@@ -100,8 +109,19 @@
         dst = win.at[2 * (1 - core) + w, :, pl.ds(first, width)]
         return remote(dst, dst, wsend.at[part, w], wrecv.at[part, w], sibling)
 
-    for copy in win_loads:
+    for copy in win_loads[:2]:
         copy.start()
+    x_load.start()
+    for copy in win_loads[2:]:
+        copy.start()
+
+    pl.semaphore_wait(barrier, len(everyone))
+
+    for copy in win_sends:
+        copy.start()
+
+    for copy in small_loads:
+        copy.wait()
 
     p0, p1, p2 = panel[0], panel[1], panel[2]
     q0 = jnp.where(p0 == LAST, p1, p0)
@@ -116,11 +136,6 @@
     lsrc[...] = jnp.where(
         cand_live, xv[:, pl.ds(pl.multiple_of(place * BLOCK, BLOCK), BLOCK)], 0.0
     )
-
-    pl.semaphore_wait(barrier, len(everyone))
-
-    for copy in win_sends:
-        copy.start()
 
     def p1_copy(d):
         to = lax.rem(y + d, N_Y)
@@ -213,57 +228,71 @@
         for d in FAR_Y:
             p5_copy(d).start()
 
+    def split(value):
+        high = value.astype(jnp.bfloat16)
+        return high, (value - high.astype(jnp.float32)).astype(jnp.bfloat16)
+
     def phase_5_end():
         for d in range(1, N_Y):
             p5_wait(d).wait_recv()
-
-    def up_copy(u):
-        return remote(up.at[u], up.at[u], up_s.at[u], up_r.at[u], above)
-
-    def down_copy(u):
-        return remote(down.at[u], down.at[u], dn_s.at[u], dn_r.at[u], below)
-
-    def sib_slot(u, half):
-        return panels.at[u, pl.ds(pl.multiple_of(half * HALF, HALF), HALF), :]
-
-    def sib_copy(u):
-        return remote(sib_slot(u, core), sib_slot(u, core), sib_s.at[u], sib_r.at[u], sibling)
-
-    def sib_wait(u):
+        left_high[...], left_low[...] = split(left[...])
+
+    def up_copy(u, h):
+        return remote(up.at[u, h], up.at[u, h], up_s.at[u, h], up_r.at[u, h], above)
+
+    def down_copy(u, h):
+        return remote(down.at[u, h], down.at[u, h], dn_s.at[u, h], dn_r.at[u, h], below)
+
+    def sib_slot(j, half):
+        rows = pl.ds(pl.multiple_of(half * HALF, HALF), HALF)
+        return panels.at[pl.ds(j * ROUNDS, ROUNDS), rows, :]
+
+    def sib_copy(j):
+        return remote(sib_slot(j, core), sib_slot(j, core), sib_s.at[j], sib_r.at[j], sibling)
+
+    def sib_wait(j):
         return remote(
-            sib_slot(u, 1 - core), sib_slot(u, 1 - core), sib_s.at[u], sib_r.at[u], sibling
+            sib_slot(j, 1 - core), sib_slot(j, 1 - core), sib_s.at[j], sib_r.at[j], sibling
         )
 
     def window_of(t):
         return jnp.where(t == 0, q[0], jnp.where(t == 1, q[1], q[2]))
 
     def slot_of(u):
-        late = u - 3 * TRIPLES
-        j = jnp.where(late < 0, u // 3, TRIPLES + jnp.maximum(late, 0) // 2)
-        t = jnp.where(late < 0, u % 3, jnp.maximum(late, 0) % 2)
+        late = jnp.maximum(u - 3 * TRIPLES, 0)
+        third = (u * 43) >> 7
+        half = late >> 1
+        early = u < 3 * TRIPLES
+        j = jnp.where(early, third, TRIPLES + half)
+        t = jnp.where(early, u - 3 * third, late - 2 * half)
         return j, t
 
     def columns(j):
         return pl.ds(pl.multiple_of(j * BLOCK, BLOCK), BLOCK)
 
-    def inject(buf, u):
-        j, t = slot_of(u)
+    def inject(buf, u, h, j, t):
         w = window_of(t)
-        value = buf[u]
+        value = buf[u, h]
         for k in range(4):
-            value = jnp.where(w == 4 * chip + k, win[k, :, columns(j)], value)
-        buf[u] = value
-
-    def wrap_copy(n):
+            own = win[k, pl.ds(h * PART, PART), columns(j)]
+            value = jnp.where(w == 4 * chip + k, own, value)
+        buf[u, h] = value
+
+    def wrap_copy(n, h):
         return remote(
-            win.at[3, :, pl.ds((DOWN_LAST + n) * BLOCK, BLOCK)], relay.at[n],
-            wr_s.at[n], rl_r.at[n], at_z(lax.rem(z + 4, N_Z)),
-        )
-
-    def relay_copy(n):
+            win.at[3, pl.ds(h * PART, PART), pl.ds((DOWN_LAST + n) * BLOCK, BLOCK)],
+            relay.at[n, h], wr_s.at[n, h], rl_r.at[n, h], at_z(lax.rem(z + 4, N_Z)),
+        )
+
+    def wrap_wait(n, h):
+        dst = relay.at[n, h]
+        return remote(dst, dst, wr_s.at[n, h], rl_r.at[n, h], at_z(lax.rem(z + 8, N_Z)))
+
+    def relay_copy(n, h):
         slot = 3 * (WRAP_FIRST + n) + 2
         return remote(
-            relay.at[n], up.at[slot], rl_s.at[n], up_r.at[slot], at_z(lax.rem(z + 3, N_Z))
+            relay.at[n, h], up.at[slot, h], rl_s.at[n, h], up_r.at[slot, h],
+            at_z(lax.rem(z + 3, N_Z)),
         )
 
     far = jnp.maximum(chip, CHIPS - 1 - chip)
@@ -273,13 +302,14 @@
         win_loads[w].wait()
         win_arrival(0, w).wait_recv()
 
+    def dot(a, b):
+        return jnp.dot(a, b, preferred_element_type=jnp.float32)
+
     def multiply(j):
-        for t in range(ROUNDS):
-            sib_wait(j * ROUNDS + t).wait_recv()
+        sib_wait(j).wait_recv()
         right = panels[pl.ds(j * ROUNDS, ROUNDS)].reshape(ROUNDS * BLOCK, BLOCK)
-        product = jnp.dot(
-            left[...], right, preferred_element_type=jnp.float32, precision=lax.Precision.HIGHEST
-        )
+        high, low = split(right)
+        product = dot(left_high[...], high) + dot(left_high[...], low) + dot(left_low[...], high)
         cols = pl.ds(pl.multiple_of(j * BLOCK, BLOCK), BLOCK)
         live = rank[0, j] < count[0, 0]
         update = jnp.where(live, 1.5 * xv[:, cols] - 0.5 * product, 0.0)
@@ -296,53 +326,56 @@
         @pl.when((s == 10) & (chip == CHIPS - 1))
         def _():
             for n in range(WRAPS):
-                wrap_copy(n).start()
-
-        for n in range(WRAPS):
-            @pl.when((s == RELAY_STEP + 2 * n) & (chip == 3))
-            def _(n=n):
-                remote(
-                    relay.at[n], relay.at[n], wr_s.at[n], rl_r.at[n], at_z(lax.rem(z + 8, N_Z))
-                ).wait_recv()
-                relay_copy(n).start()
+                for h in range(SUB):
+                    wrap_copy(n, h).start()
+
+        @pl.when((s >= RELAY_STEP) & (s < RELAY_STEP + WRAPS) & (chip == 3))
+        def _():
+            n = s - RELAY_STEP
+            for h in range(SUB):
+                wrap_wait(n, h).wait_recv()
+                relay_copy(n, h).start()
 
         u = s - chip * LAG
         uj, ut = slot_of(jnp.clip(u, 0, SLOTS - 1))
 
         @pl.when((u >= 0) & (u < SLOTS) & (ut < 2))
         def _():
-            @pl.when(chip > 0)
-            def _():
-                up_copy(u).wait_recv()
-
-            inject(up, u)
-
-            @pl.when(chip < CHIPS - 1)
-            def _():
-                up_copy(u).start()
+            for h in range(SUB):
+                @pl.when(chip > 0)
+                def _():
+                    up_copy(u, h).wait_recv()
+
+                inject(up, u, h, uj, ut)
+
+                @pl.when(chip < CHIPS - 1)
+                def _():
+                    up_copy(u, h).start()
 
         @pl.when((u >= 0) & (u < SLOTS) & (ut == 2) & (uj >= WRAP_FIRST) & (chip < CHIPS - 1))
         def _():
-            up_copy(u).wait_recv()
-
-            @pl.when(chip < CHIPS - 2)
-            def _():
-                up_copy(u).start()
+            for h in range(SUB):
+                up_copy(u, h).wait_recv()
+
+                @pl.when(chip < CHIPS - 2)
+                def _():
+                    up_copy(u, h).start()
 
         d = s - (CHIPS - 1 - chip) * LAG
         dj, dt = slot_of(jnp.clip(d, 0, SLOTS - 1))
 
         @pl.when((d >= 0) & (d < SLOTS) & ((dt < 2) | (dj < DOWN_LAST)))
         def _():
-            @pl.when(chip < CHIPS - 1)
-            def _():
-                down_copy(d).wait_recv()
-
-            inject(down, d)
-
-            @pl.when(chip > 0)
-            def _():
-                down_copy(d).start()
+            for h in range(SUB):
+                @pl.when(chip < CHIPS - 1)
+                def _():
+                    down_copy(d, h).wait_recv()
+
+                inject(down, d, h, dj, dt)
+
+                @pl.when(chip > 0)
+                def _():
+                    down_copy(d, h).start()
 
         f = s - far * LAG
 
@@ -351,18 +384,22 @@
         def finish(j, t, value):
             unit = ROUNDS * j + t
             panels[unit, pl.ds(pl.multiple_of(core * HALF, HALF), HALF), :] = value
-            sib_copy(unit).start()
 
         @pl.when((f >= 0) & (f < SLOTS) & ((ft < 2) | (fj < DOWN_LAST)))
         def _():
-            finish(fj, ft, jnp.where(window_of(ft) // 4 < chip, up[f], down[f]))
+            value = jnp.where(window_of(ft) // 4 < chip, up[f], down[f])
+            finish(fj, ft, value.reshape(HALF, BLOCK))
+
+            @pl.when(ft == jnp.where(fj < DOWN_LAST, 2, 1))
+            def _():
+                sib_copy(fj).start()
 
         wraps = (f >= 0) & (f < SLOTS) & (ft == 2) & (fj >= WRAP_FIRST)
         wrapped = fj + DOWN_LAST - WRAP_FIRST
 
         @pl.when(wraps & (chip < CHIPS - 1))
         def _():
-            finish(wrapped, 2, up[f])
+            finish(wrapped, 2, up[f].reshape(HALF, BLOCK))
 
         @pl.when(wraps & (chip == CHIPS - 1))
         def _():
@@ -425,11 +462,13 @@
             (chip < CHIPS - 1) & (t < 2) | (chip < CHIPS - 2) & (t == 2) & (j >= WRAP_FIRST)
         )
         def _():
-            up_copy(u).wait_send()
+            for h in range(SUB):
+                up_copy(u, h).wait_send()
 
         @pl.when((chip > 0) & ((t < 2) | (j < DOWN_LAST)))
         def _():
-            down_copy(u).wait_send()
+            for h in range(SUB):
+                down_copy(u, h).wait_send()
 
         return carry
 
@@ -439,15 +478,17 @@
         sib_copy(u).wait_send()
         return carry
 
-    lax.fori_loop(0, UNITS, drain_sib, 0)
+    lax.fori_loop(0, TILE_COLS, drain_sib, 0)
     for n in range(WRAPS):
         @pl.when(chip == CHIPS - 1)
         def _(n=n):
-            wrap_copy(n).wait_send()
+            for h in range(SUB):
+                wrap_copy(n, h).wait_send()
 
         @pl.when(chip == 3)
         def _(n=n):
-            relay_copy(n).wait_send()
+            for h in range(SUB):
+                relay_copy(n, h).wait_send()
 
     for d in range(1, N_Z):
         frm = lax.rem(z + N_Z - d, N_Z)
@@ -478,6 +519,27 @@
     store.wait()
 
 
+def hand_over(updated, total, updated_out, total_out, held, sems):
+    rows = BLOCK // 4
+    parts = [pl.ds(n * rows, rows) for n in range(4)]
+    loads = [
+        pltpu.make_async_copy(updated.at[part], held.at[part], sems.at[0, n])
+        for n, part in enumerate(parts)
+    ]
+    stores = [
+        pltpu.make_async_copy(held.at[part], updated_out.at[part], sems.at[1, n])
+        for n, part in enumerate(parts)
+    ]
+    for load in loads:
+        load.start()
+    total_out[0, 0] = total[0, 0]
+    for load, store in zip(loads, stores):
+        load.wait()
+        store.start()
+    for store in stores:
+        store.wait()
+
+
 def on_device(x_window, square_rows, block_rank, block_count, panel_order):
     width = TILE_COLS * BLOCK
     vmem = lambda *shape: pltpu.VMEM(shape, jnp.float32)
@@ -488,18 +550,20 @@
             jax.ShapeDtypeStruct((BLOCK, width), jnp.float32),
             jax.ShapeDtypeStruct((1, 1), jnp.float32),
         ),
-        in_specs=[pl.BlockSpec(memory_space=pltpu.SMEM)] * 3
-        + [pl.BlockSpec(memory_space=pl.ANY)] * 2,
+        in_specs=[pl.BlockSpec(memory_space=pl.ANY)] * 5,
         out_specs=(
             pl.BlockSpec(memory_space=pl.ANY),
             pl.BlockSpec(memory_space=pltpu.SMEM),
         ),
         scratch_shapes=[
+            pltpu.SMEM((ROUNDS,), jnp.int32),
+            pltpu.SMEM((1, TILE_COLS), jnp.int32),
+            pltpu.SMEM((1, 1), jnp.int32),
             vmem(BLOCK, width),
             vmem(4, HALF, width),
-            vmem(SLOTS, HALF, BLOCK),
-            vmem(SLOTS, HALF, BLOCK),
-            vmem(WRAPS, HALF, BLOCK),
+            vmem(SLOTS, SUB, PART, BLOCK),
+            vmem(SLOTS, SUB, PART, BLOCK),
+            vmem(WRAPS, SUB, PART, BLOCK),
             vmem(UNITS, BLOCK, BLOCK),
             vmem(BLOCK, width),
             vmem(BLOCK, BLOCK),
@@ -510,14 +574,16 @@
             vmem(PIECE, BLOCK),
             vmem(PIECE, ROUNDS * BLOCK),
             vmem(BLOCK, ROUNDS * BLOCK),
+            pltpu.VMEM((BLOCK, ROUNDS * BLOCK), jnp.bfloat16),
+            pltpu.VMEM((BLOCK, ROUNDS * BLOCK), jnp.bfloat16),
             vmem(8, BLOCK),
             vmem(1, 8, BLOCK),
             vmem(N_Z, 8, BLOCK),
             vmem(N_Y, 8, BLOCK),
             vmem(N_X, 8, BLOCK),
-            dma(2), dma(2, 2), dma(2, 2), dma(2, 2),
-            dma(SLOTS), dma(SLOTS), dma(SLOTS), dma(SLOTS),
-            dma(WRAPS), dma(WRAPS), dma(WRAPS), dma(UNITS), dma(UNITS),
+            dma(3), dma(2), dma(2, 2), dma(2, 2), dma(2, 2),
+            dma(SLOTS, SUB), dma(SLOTS, SUB), dma(SLOTS, SUB), dma(SLOTS, SUB),
+            dma(WRAPS, SUB), dma(WRAPS, SUB), dma(WRAPS, SUB), dma(TILE_COLS), dma(TILE_COLS),
             dma(N_Y - 1), dma(N_Y - 1), dma(ROUNDS), dma(N_X), dma(1), dma(1),
             dma(N_X - 1), dma(N_X - 1), dma(N_Y - 1), dma(N_Y - 1),
             dma(1), dma(1), dma(N_Z - 1), dma(N_Z - 1),
@@ -528,6 +594,21 @@
         ),
         name="sign_window",
     )(panel_order, block_rank, block_count, x_window, square_rows)
+    updated, total = pl.pallas_call(
+        hand_over,
+        out_shape=(
+            jax.ShapeDtypeStruct((BLOCK, width), jnp.float32),
+            jax.ShapeDtypeStruct((1, 1), jnp.float32),
+        ),
+        in_specs=[pl.BlockSpec(memory_space=pl.ANY), pl.BlockSpec(memory_space=pltpu.SMEM)],
+        out_specs=(
+            pl.BlockSpec(memory_space=pl.ANY),
+            pl.BlockSpec(memory_space=pltpu.SMEM),
+        ),
+        scratch_shapes=[vmem(BLOCK, width), dma(2, 4)],
+        compiler_params=pltpu.CompilerParams(vmem_limit_bytes=62 << 20),
+        name="hand_over",
+    )(updated, total)
     return updated, total[0, 0]
 
 

time: 93.9 us -> 91.8 us (0.978)
  Pallas kernels: 87.5 us -> 90 us
  local copies, waits for them, and re-layouts: 2.21 us -> 0 us
  between operations: 2.96 us -> 1.29 us
    pallas_call x0 -> x1, Pallas kernels: none -> 3.14 us  [on_device(): pl.pallas_call(hand_over, out_shape=(jax.ShapeDtypeStruct((BLOCK, width),...]
    unnamed x1 -> x0, local copies, waits for them, and re-layouts: 2.21 us -> none
where the time goes in v3:
time: 91.8 us; the launch traced here: 91.3 us
  Pallas kernels  90 us (98%)
  between operations  1.29 us (1%)
    pallas_call x1, Pallas kernels, on_device(): pl.pallas_call(kernel, out_shape=(jax.ShapeDtypeStruct((BLOCK, width), jn...  86.8 us
    pallas_call x1, Pallas kernels, on_device(): pl.pallas_call(hand_over, out_shape=(jax.ShapeDtypeStruct((BLOCK, width),...  3.14 us

profile of v3, /device:TPU:1, one launch (start us, length us, event | category | flops | bytes accessed | tf_op | source)
XLA Modules:
  0.0 91.3 jit_solution(4728933213014489562)
XLA Ops:
  1.3 86.8 %sign_window.1 = (f32[128,1920]{1,0:T(8,128)}, f32[1,1]{1,0:T(1,128)}) custom-call(s32[3]{0:T(128)} %panel_hbm.1, s32[1,15]{1,0:T(1,128)} %rank_hbm.1, s32[1,1]{1,0:T(1,128)S(6)} %copy.7.count_hbm, f32[128,1920]{1,0:T(8,128)} %x_hbm.1, f32[256,1920]{1,0:T(8,128)} %sq_hbm.1), custom_call_target="tpu_custom_call" | custom-call | tf_op jit(solution)/shard_map/sign_window/pallas_call | solution.py:547
  88.1 3.1 %hand_over.1 = (f32[128,1920]{1,0:T(8,128)}, f32[1,1]{1,0:T(1,128)}) custom-call(f32[128,1920]{1,0:T(8,128)} %get-tuple-element.6.updated, f32[1,1]{1,0:T(1,128)} %get-tuple-element.7.total), custom_call_target="tpu_custom_call" | custom-call | tf_op jit(solution)/shard_map/hand_over/pallas_call | solution.py:597
